TPU v7x, 256 devices: a whole 4x4x8 slice. The times are simulated.
256 devices in a mesh: seq: 32 (over z, x), req: 8 (over y, core).
Axes of the slice: x: 4, y: 4, z: 8, core: 2. Of those that a mesh axis runs over, the one named last changes fastest.
Arguments:
- tokens: bfloat16 [64, 4, 2048], P('req'), may hold values from -6 to 6
- lengths: int32 [64], P('req'), may hold values from 1 to 2044, as said below
- cache_keys: bfloat16 [64, 2048, 2048], P('req', 'seq'), may hold values from -120 to 120
- cache_values: bfloat16 [64, 2048, 2048], P('req', 'seq'), may hold values from -6 to 6
- norm1_gain: float32 [2048], replicated, may hold values from 0.5 to 1.5
- norm1_bias: float32 [2048], replicated, may hold values from -1.75 to 1.75
- w_query: bfloat16 [2048, 2048], P('req', 'seq'), may hold values from -0.125 to 0.125
- b_query: float32 [2048], P('seq'), may hold values from -3 to 3
- w_key: bfloat16 [2048, 2048], P('req', 'seq'), may hold values from -0.125 to 0.125
- b_key: float32 [2048], P('seq'), may hold values from -3 to 3
- w_value: bfloat16 [2048, 2048], P('req', 'seq'), may hold values from -0.125 to 0.125
- b_value: float32 [2048], P('seq'), may hold values from -3 to 3
- w_out: bfloat16 [2048, 2048], P('req', 'seq'), may hold values from -0.125 to 0.125
- b_out: float32 [2048], P('seq'), may hold values from -3 to 3
- norm2_gain: float32 [2048], replicated, may hold values from 0.5 to 1.5
- norm2_bias: float32 [2048], replicated, may hold values from -1.75 to 1.75
- w_up: bfloat16 [2048, 8192], P('req', 'seq'), may hold values from -0.125 to 0.125
- b_up: float32 [8192], P('seq'), may hold values from -3 to 3
- w_down: bfloat16 [8192, 2048], P('seq', 'req'), may hold values from -0.0625 to 0.0625
- b_down: float32 [2048], replicated, may hold values from -3 to 3
Outputs:
- hidden_out: bfloat16 [64, 4, 2048], P('req')
- new_keys: bfloat16 [64, 2048, 2048], P('req', 'seq')
- new_values: bfloat16 [64, 2048, 2048], P('req', 'seq')
Inputs may be any that keep to these rules, and one draw needn't show every extreme that they name: `lengths`: one request has exactly 2044 cached positions.
All inputs are finite; a program needn't handle non-finite values.
Results may differ from a plain program's by a relative error of at most 0.033.
Values may be sent and summed in bfloat16 or wider, within the bound.
A program may use at most 64 MiB of HBM per device.

v0:
```python
import jax
import jax.numpy as jnp
from jax import lax
from jax.sharding import PartitionSpec as P

HEADS = 16
HEAD = 128


def merged(x, axis, combine):
    everything = jax.tree.map(
        lambda part, kind: lax.all_gather(part.astype(kind), axis),
        x,
        (jnp.bfloat16, jnp.bfloat16, jnp.bfloat16),
    )

    def take(k):
        return jax.tree.map(lambda part, own: part[k].astype(own.dtype), everything, x)

    return lax.fori_loop(
        1, lax.axis_size(axis), lambda k, so_far: combine(so_far, take(k)), take(0)
    )


def layer_norm(values, gain, shift):
    center = values - jnp.mean(values, axis=-1, keepdims=True)
    spread = jnp.mean(center * center, axis=-1, keepdims=True)
    return center * lax.rsqrt(spread + 1e-05) * gain + shift


def combine(first, second):
    peak_a, total_a, part_a = first
    peak_b, total_b, part_b = second
    peak = jnp.maximum(peak_a, peak_b)
    scale_a = jnp.exp(peak_a - peak)
    scale_b = jnp.exp(peak_b - peak)
    total = total_a * scale_a + total_b * scale_b
    part = part_a * scale_a[..., None] + part_b * scale_b[..., None]
    return (peak, total, part)


def body(
    tokens,
    lengths,
    cache_keys,
    cache_values,
    norm1_gain,
    norm1_bias,
    w_query,
    b_query,
    w_key,
    b_key,
    w_value,
    b_value,
    w_out,
    b_out,
    norm2_gain,
    norm2_bias,
    w_up,
    b_up,
    w_down,
    b_down,
):
    group = tokens.shape[0]
    residual = tokens.astype(jnp.float32)
    normed = layer_norm(residual, norm1_gain, norm1_bias).astype(jnp.bfloat16)
    full_query, full_key, full_value, full_out, full_up = (
        lax.all_gather(w_query, "req", axis=0, tiled=True),
        lax.all_gather(w_key, "req", axis=0, tiled=True),
        lax.all_gather(w_value, "req", axis=0, tiled=True),
        lax.all_gather(w_out, "req", axis=0, tiled=True),
        lax.all_gather(w_up, "req", axis=0, tiled=True),
    )
    query_cols = (jnp.dot(normed, full_query, preferred_element_type=jnp.float32) + b_query).astype(
        jnp.bfloat16
    )
    key_cols = (jnp.dot(normed, full_key, preferred_element_type=jnp.float32) + b_key).astype(
        jnp.bfloat16
    )
    value_cols = (jnp.dot(normed, full_value, preferred_element_type=jnp.float32) + b_value).astype(
        jnp.bfloat16
    )
    query, key_rows, value_rows = (
        lax.all_gather(query_cols, "seq", axis=2, tiled=True),
        lax.all_gather(key_cols, "seq", axis=2, tiled=True),
        lax.all_gather(value_cols, "seq", axis=2, tiled=True),
    )
    steps, width = (query.shape[1], query.shape[2])
    slots = cache_keys.shape[1]
    position = lax.axis_index("seq") * slots + jnp.arange(slots, dtype=jnp.int32)
    new_keys = cache_keys
    new_values = cache_values
    for step in range(steps):
        hit = (position[None, :] == lengths[:, None] + step)[:, :, None]
        new_keys = jnp.where(hit, key_rows[:, step][:, None, :], new_keys)
        new_values = jnp.where(hit, value_rows[:, step][:, None, :], new_values)
    query_heads = query.reshape(group, steps, HEADS, HEAD)
    key_heads = new_keys.reshape(group, slots, HEADS, HEAD)
    value_heads = new_values.reshape(group, slots, HEADS, HEAD)
    scores = jnp.einsum(
        "rthd,rshd->rths", query_heads, key_heads, preferred_element_type=jnp.float32
    ) * HEAD ** (-0.5)
    limit = lengths[:, None] + jnp.arange(steps, dtype=jnp.int32)[None, :]
    valid = position[None, None, None, :] <= limit[:, :, None, None]
    masked = jnp.where(valid, scores, -1e30)
    peak = jnp.max(masked, axis=-1)
    expo = jnp.where(valid, jnp.exp(masked - peak[..., None]), 0.0)
    total = jnp.sum(expo, axis=-1)
    partial_value = jnp.einsum(
        "rths,rshd->rthd",
        expo.astype(jnp.bfloat16),
        value_heads,
        preferred_element_type=jnp.float32,
    )
    peak, total, partial_value = merged((peak, total, partial_value), "seq", combine)
    attn = (partial_value / total[..., None]).reshape(group, steps, width).astype(jnp.bfloat16)
    out_part = (jnp.dot(attn, full_out, preferred_element_type=jnp.float32) + b_out).astype(
        jnp.bfloat16
    )
    projected = lax.all_gather(out_part, "seq", axis=2, tiled=True)
    mid = residual + projected.astype(jnp.float32)
    normed2 = layer_norm(mid, norm2_gain, norm2_bias).astype(jnp.bfloat16)
    hidden = jax.nn.gelu(
        jnp.dot(normed2, full_up, preferred_element_type=jnp.float32) + b_up, approximate=False
    ).astype(jnp.bfloat16)
    feed = jnp.dot(
        hidden,
        lax.all_gather(w_down, "req", axis=1, tiled=True),
        preferred_element_type=jnp.float32,
    )
    summed = lax.psum(feed.astype(jnp.bfloat16), "seq").astype(jnp.float32)
    hidden_out = (mid + summed + b_down).astype(jnp.bfloat16)
    return (hidden_out, new_keys, new_values)


def solution(mesh):
    in_specs = (
        P("req", None, None),
        P("req"),
        P("req", "seq", None),
        P("req", "seq", None),
        P(),
        P(),
        P("req", "seq"),
        P("seq"),
        P("req", "seq"),
        P("seq"),
        P("req", "seq"),
        P("seq"),
        P("req", "seq"),
        P("seq"),
        P(),
        P(),
        P("req", "seq"),
        P("seq"),
        P("seq", "req"),
        P(),
    )
    out_specs = (P("req", None, None), P("req", "seq", None), P("req", "seq", None))
    return jax.shard_map(body, mesh=mesh, in_specs=in_specs, out_specs=out_specs, check_vma=False)
```

profile of v0, /device:TPU:2, one launch (start us, length us, event | category | flops | bytes accessed | tf_op | source)
XLA Modules:
  0.0 581.9 jit_solution(13199156575693389009)
XLA Ops:
  10.8 13.6 %all_gather.50 = bf16[2048,64]{0,1:T(8,128)(2,1)S(1)} all-gather(bf16[256,64]{0,1:T(8,128)(2,1)} %param.32), channel_id=1, replica_groups=mesh['seq'=32,'req'=8] {'req'}, dimensions={0}, use_global_device_ids=true | all-gather | bytes 294912 | tf_op jit(solution)/shard_map/all_gather | solution.py:70
  24.4 1.2 fusion.26
  25.7 54.4 %all_gather.51 = bf16[8,4,2048]{0,1,2:T(4,128)(2,1)S(1)} all-gather(bf16[8,4,64]{0,1,2:T(4,128)(2,1)S(1)} %copy.89), channel_id=1, replica_groups=mesh['seq'=32,'req'=8] {'seq'}, dimensions={2}, use_global_device_ids=true | all-gather | bytes 135168 | tf_op jit(solution)/shard_map/all_gather | solution.py:86
  80.1 3.8 fusion.133
  83.9 2.2 copy.105
  87.7 12.8 %all_gather.44 = bf16[2048,64]{0,1:T(8,128)(2,1)S(1)} all-gather(bf16[256,64]{0,1:T(8,128)(2,1)S(1)} %copy-done.3), channel_id=1, replica_groups=mesh['seq'=32,'req'=8] {'req'}, dimensions={0}, use_global_device_ids=true | all-gather | bytes 294912 | tf_op jit(solution)/shard_map/all_gather | solution.py:69
  100.9 50.0 %all_gather.45 = bf16[8,4,2048]{0,1,2:T(4,128)(2,1)S(1)} all-gather(bf16[8,4,64]{0,1,2:T(4,128)(2,1)S(1)} %copy.76), channel_id=1, replica_groups=mesh['seq'=32,'req'=8] {'seq'}, dimensions={2}, use_global_device_ids=true | all-gather | bytes 135168 | tf_op jit(solution)/shard_map/all_gather | solution.py:85
  151.0 3.8 fusion.134
  154.8 2.2 copy.101
  158.5 12.8 %all_gather.46 = bf16[2048,64]{0,1:T(8,128)(2,1)S(1)} all-gather(bf16[256,64]{0,1:T(8,128)(2,1)S(1)} %copy-done.4), channel_id=1, replica_groups=mesh['seq'=32,'req'=8] {'req'}, dimensions={0}, use_global_device_ids=true | all-gather | bytes 294912 | tf_op jit(solution)/shard_map/all_gather | solution.py:68
  171.7 50.1 %all_gather.47 = bf16[8,4,2048]{0,1,2:T(4,128)(2,1)S(1)} all-gather(bf16[8,4,64]{0,1,2:T(4,128)(2,1)S(1)} %copy.81), channel_id=1, replica_groups=mesh['seq'=32,'req'=8] {'seq'}, dimensions={2}, use_global_device_ids=true | all-gather | bytes 135168 | tf_op jit(solution)/shard_map/all_gather | solution.py:84
  223.0 2.9 select_select_fusion
  226.0 1.3 fusion.135
  231.1 47.5 %all-gather.1 = bf16[256,4,16]{2,1,0:T(4,128)(2,1)S(1)} all-gather(bf16[8,4,16]{2,1,0:T(4,128)(2,1)S(1)} %copy.88), channel_id=3, replica_groups=mesh['seq'=32,'req'=8] {'seq'}, dimensions={0}, use_global_device_ids=true | all-gather | bytes 33792 | tf_op jit(solution)/shard_map/all_gather | solution.py:12
  278.6 47.5 %all-gather = bf16[256,4,16]{2,1,0:T(4,128)(2,1)S(1)} all-gather(bf16[8,4,16]{2,1,0:T(4,128)(2,1)S(1)} %copy.86), channel_id=2, replica_groups=mesh['seq'=32,'req'=8] {'seq'}, dimensions={0}, use_global_device_ids=true | all-gather | bytes 33792 | tf_op jit(solution)/shard_map/all_gather | solution.py:12
  326.1 12.8 %all_gather.54 = bf16[2048,64]{0,1:T(8,128)(2,1)S(1)} all-gather(bf16[256,64]{0,1:T(8,128)(2,1)S(1)} %copy-done.5), channel_id=1, replica_groups=mesh['seq'=32,'req'=8] {'req'}, dimensions={0}, use_global_device_ids=true | all-gather | bytes 294912 | tf_op jit(solution)/shard_map/all_gather | solution.py:71
  339.9 38.4 %while.19 = (s32[]{:T(128)}, f32[8,4,16]{2,1,0:T(4,128)S(1)}, f32[8,4,16]{2,1,0:T(4,128)S(1)}, f32[8,4,16,128]{3,2,1,0:T(8,128)S(1)}, bf16[32,8,4,16]{3,2,1,0:T(...) while((s32[]{:T(128)}, f32[8,4,16]{2,1,0:T(4,128)S(1)}, ...), condition=%wide.region_5.6_spmd, body=%wide.region_4.5_spmd.sunk | while | flops 266245 | bytes 673943 | solution.py:20
  339.9 1.2 fusion.143
  341.2 1.2 fusion.143
  342.4 1.2 fusion.143
  343.6 1.2 fusion.143
  344.9 1.2 fusion.143
  346.1 1.2 fusion.143
  347.4 1.2 fusion.143
  348.6 1.2 fusion.143
  349.8 1.2 fusion.143
  351.1 1.2 fusion.143
  352.3 1.2 fusion.143
  353.5 1.2 fusion.143
  354.8 1.2 fusion.143
  356.0 1.2 fusion.143
  357.3 1.2 fusion.143
  358.5 1.2 fusion.143
  359.8 1.2 fusion.143
  361.0 1.2 fusion.143
  362.2 1.2 fusion.143
  363.5 1.2 fusion.143
  364.7 1.2 fusion.143
  365.9 1.2 fusion.143
  367.2 1.2 fusion.143
  368.4 1.2 fusion.143
  369.6 1.2 fusion.143
  372.1 1.2 fusion.143
  373.4 1.2 fusion.143
  378.8 50.4 %all_gather.55 = bf16[8,4,2048]{0,1,2:T(4,128)(2,1)S(1)} all-gather(bf16[8,4,64]{0,1,2:T(4,128)(2,1)S(1)} %copy.96), channel_id=1, replica_groups=mesh['seq'=32,'req'=8] {'seq'}, dimensions={2}, use_global_device_ids=true | all-gather | bytes 135168 | tf_op jit(solution)/shard_map/all_gather | solution.py:120
  430.9 1.6 fusion.94
  432.5 2.2 convolution_convert_fusion
  434.7 138.8 %all-reduce.2.cloned.1.call-done = bf16[8,4,2048]{2,0,1:T(8,128)(2,1)} async-done(((bf16[8,4,2048]{2,0,1:T(8,128)(2,1)}), bf16[8,4,2048]{2,0,1:T(8,128)(2,1)}) %all-reduce.2.cloned.1.call-update) | async-done | bytes 131088 | tf_op jit(solution)/shard_map/psum | solution.py:131
  (120 shorter events, 23.3 us)
Async XLA Ops:
  7.2 331.8 %all-gather.11.cloned.1.call-start = ((), (), s32[]{:S(2)}) async-start(), calls=%async_computation.3 | async-start | bytes 4325376 | tf_op jit(solution)/shard_map/all_gather | solution.py:12
  83.9 3.7 copy-start.3
  83.9 16.6 %copy-start = (bf16[8,4,2048]{2,1,0:T(4,128)(2,1)S(1)}, bf16[8,4,2048]{2,1,0:T(4,128)(2,1)}, u32[]{:S(2)}) copy-start(bf16[8,4,2048]{2,1,0:T(4,128)(2,1)} %param.22) | copy-start | bytes 393220
  83.9 16.6 %copy-start.11 = (f32[2048]{0:T(1024)S(1)}, f32[2048]{0:T(1024)}, u32[]{:S(2)}) copy-start(f32[2048]{0:T(1024)} %param.27) | copy-start | bytes 24580
  83.9 16.6 %copy-start.12 = (f32[2048]{0:T(1024)S(1)}, f32[2048]{0:T(1024)}, u32[]{:S(2)}) copy-start(f32[2048]{0:T(1024)} %param.26) | copy-start | bytes 24580
  83.9 16.6 %copy-start.13 = (f32[64]{0:T(128)S(1)}, f32[64]{0:T(128)}, u32[]{:S(2)}) copy-start(f32[64]{0:T(128)} %param.31) | copy-start | bytes 772
  154.8 3.7 copy-start.4
  154.8 16.5 %copy-start.14 = (f32[64]{0:T(128)S(1)}, f32[64]{0:T(128)}, u32[]{:S(2)}) copy-start(f32[64]{0:T(128)} %param.29) | copy-start | bytes 772
  171.7 51.2 %copy-start.9 = (s32[8]{0:T(128)S(1)}, s32[8]{0:T(128)}, u32[]{:S(2)}) copy-start(s32[8]{0:T(128)} %param.23) | copy-start | bytes 100
  226.0 2.0 copy-start.1
  226.0 2.0 copy-start.2
  227.2 98.8 %copy-start.5 = (bf16[256,64]{0,1:T(8,128)(2,1)S(1)}, bf16[256,64]{0,1:T(8,128)(2,1)}, u32[]{:S(2)}) copy-start(bf16[256,64]{0,1:T(8,128)(2,1)} %param.34) | copy-start | bytes 98308
  228.7 202.2 %all-gather.7.cloned.1.call-start = ((), (), s32[]{:S(2)}) async-start(), calls=%async_computation | async-start | bytes 1179648 | tf_op jit(solution)/shard_map/all_gather | solution.py:72
  229.5 203.0 %all-gather.9.cloned.1.call-start = ((), (), s32[]{:S(2)}) async-start(), calls=%async_computation.1 | async-start | bytes 1179648 | tf_op jit(solution)/shard_map/all_gather | solution.py:128
  230.2 343.4 %all-reduce.2.cloned.1.call-start = ((), (), s32[]{:S(2)}) async-start(), calls=%async_computation.2 | async-start | bytes 262144 | tf_op jit(solution)/shard_map/psum | solution.py:131
  339.9 38.6 %copy-start.15 = (f32[64]{0:T(128)S(1)}, f32[64]{0:T(128)}, u32[]{:S(2)}) copy-start(f32[64]{0:T(128)} %param.35) | copy-start | bytes 772
  378.8 52.1 %copy-start.6 = (f32[2048]{0:T(1024)S(1)}, f32[2048]{0:T(1024)}, u32[]{:S(2)}) copy-start(f32[2048]{0:T(1024)} %param.37) | copy-start | bytes 24580
  378.8 52.1 %copy-start.7 = (f32[2048]{0:T(1024)S(1)}, f32[2048]{0:T(1024)}, u32[]{:S(2)}) copy-start(f32[2048]{0:T(1024)} %param.36) | copy-start | bytes 24580
  378.8 52.1 %copy-start.10 = (f32[256]{0:T(256)S(1)}, f32[256]{0:T(256)}, u32[]{:S(2)}) copy-start(f32[256]{0:T(256)} %param.39) | copy-start | bytes 3076
  430.4 143.1 %copy-start.8 = (f32[2048]{0:T(1024)S(1)}, f32[2048]{0:T(1024)}, u32[]{:S(2)}) copy-start(f32[2048]{0:T(1024)} %param.41) | copy-start | bytes 24580
Sparse Core Ops, SparseCore 0:
  228.8 78.4 all-gather.10
  309.2 24.8 all-gather.6
  335.9 25.9 all-gather.8
  434.9 138.6 all-reduce.1
where the time goes:
time: 583 us; the launch traced here: 582 us
  blocking collectives  352 us (60%)
  waiting for transfers between devices  140 us (24%)
  other arithmetic  47.2 us (8%)
  local copies, waits for them, and re-layouts  19.5 us (3%)
  between operations  14.1 us (2%)
  matrix products  7.72 us (1%)
    psum x1, waiting for transfers between devices, body(): summed = lax.psum(feed.astype(jnp.bfloat16), 'seq').astype(jnp.float32)  139 us
    all_gather x2, blocking collectives, merged(): lax.all_gather(part.astype(kind), axis)  94.9 us
    all_gather x1, blocking collectives, body(): lax.all_gather(value_cols, 'seq', axis=2, tiled=True)  54.4 us
    all_gather x1, blocking collectives, body(): projected = lax.all_gather(out_part, 'seq', axis=2, tiled=True)  50.4 us
    all_gather x1, blocking collectives, body(): lax.all_gather(query_cols, 'seq', axis=2, tiled=True)  50.1 us
    all_gather x1, blocking collectives, body(): lax.all_gather(key_cols, 'seq', axis=2, tiled=True)  50 us
    add x31, other arithmetic, combine(): part = part_a * scale_a[..., None] + part_b * scale_b[..., None]  36.3 us
    all_gather x1, blocking collectives, body(): lax.all_gather(w_value, 'req', axis=0, tiled=True)  13.6 us
  transfers between devices with their start and end apart: 4, of which 1 were waited for; matrix products, arithmetic and copies ran while one was open for 7% of the time, Pallas kernels for 0%

commit v1 on v0

--- a/solution.py
+++ b/solution.py
@@ -128,7 +128,7 @@
         lax.all_gather(w_down, "req", axis=1, tiled=True),
         preferred_element_type=jnp.float32,
     )
-    summed = lax.psum(feed.astype(jnp.bfloat16), "seq").astype(jnp.float32)
+    summed = jnp.sum(lax.all_gather(feed.astype(jnp.bfloat16), "seq"), axis=0).astype(jnp.float32)
     hidden_out = (mid + summed + b_down).astype(jnp.bfloat16)
     return (hidden_out, new_keys, new_values)
 

time: 583 us -> 526 us (0.902)
  waiting for transfers between devices: 140 us -> 80 us
    psum x1 -> x0, waiting for transfers between devices: 139 us -> none  [body(): summed = lax.psum(feed.astype(jnp.bfloat16), 'seq').astype(jnp.float32)]
    all_gather x0 -> x1, waiting for transfers between devices: none -> 78.5 us  [body(): lax.all_gather(feed.astype(jnp.bfloat16), 'seq')]
  transfers between devices with their start and end apart: 4 -> 4, of which waited for: 1 -> 1; matrix products, arithmetic and copies ran while one was open for 7% -> 8% of each run, Pallas kernels for 0% -> 0%
where the time goes in v1:
time: 526 us; the launch traced here: 524 us
  blocking collectives  352 us (67%)
  waiting for transfers between devices  80 us (15%)
  other arithmetic  49.2 us (9%)
  local copies, waits for them, and re-layouts  19.5 us (4%)
  between operations  14.1 us (3%)
  matrix products  7.72 us (1%)
    all_gather x2, blocking collectives, merged(): lax.all_gather(part.astype(kind), axis)  94.9 us
    all_gather x1, waiting for transfers between devices, body(): lax.all_gather(feed.astype(jnp.bfloat16), 'seq')  78.5 us
    all_gather x1, blocking collectives, body(): lax.all_gather(value_cols, 'seq', axis=2, tiled=True)  54.4 us
    all_gather x1, blocking collectives, body(): projected = lax.all_gather(out_part, 'seq', axis=2, tiled=True)  50.4 us
    all_gather x1, blocking collectives, body(): lax.all_gather(query_cols, 'seq', axis=2, tiled=True)  50.1 us
    all_gather x1, blocking collectives, body(): lax.all_gather(key_cols, 'seq', axis=2, tiled=True)  50 us
    add x31, other arithmetic, combine(): part = part_a * scale_a[..., None] + part_b * scale_b[..., None]  36.3 us
    all_gather x1, blocking collectives, body(): lax.all_gather(w_value, 'req', axis=0, tiled=True)  13.6 us
  transfers between devices with their start and end apart: 4, of which 1 were waited for; matrix products, arithmetic and copies ran while one was open for 8% of the time, Pallas kernels for 0%

profile of v1, /device:TPU:2, one launch (start us, length us, event | category | flops | bytes accessed | tf_op | source)
XLA Modules:
  0.0 523.6 jit_solution(743119763912550425)
XLA Ops:
  10.8 13.6 %all_gather.56 = bf16[2048,64]{0,1:T(8,128)(2,1)S(1)} all-gather(bf16[256,64]{0,1:T(8,128)(2,1)} %param.32), channel_id=1, replica_groups=mesh['seq'=32,'req'=8] {'req'}, dimensions={0}, use_global_device_ids=true | all-gather | bytes 294912 | tf_op jit(solution)/shard_map/all_gather | solution.py:70
  24.4 1.2 fusion.26
  25.7 54.4 %all_gather.57 = bf16[8,4,2048]{0,1,2:T(4,128)(2,1)S(1)} all-gather(bf16[8,4,64]{0,1,2:T(4,128)(2,1)S(1)} %copy.117), channel_id=1, replica_groups=mesh['seq'=32,'req'=8] {'seq'}, dimensions={2}, use_global_device_ids=true | all-gather | bytes 135168 | tf_op jit(solution)/shard_map/all_gather | solution.py:86
  80.1 3.8 fusion.133
  83.9 2.2 copy.133
  87.7 12.8 %all_gather.50 = bf16[2048,64]{0,1:T(8,128)(2,1)S(1)} all-gather(bf16[256,64]{0,1:T(8,128)(2,1)S(1)} %copy-done.3), channel_id=1, replica_groups=mesh['seq'=32,'req'=8] {'req'}, dimensions={0}, use_global_device_ids=true | all-gather | bytes 294912 | tf_op jit(solution)/shard_map/all_gather | solution.py:69
  100.9 50.0 %all_gather.51 = bf16[8,4,2048]{0,1,2:T(4,128)(2,1)S(1)} all-gather(bf16[8,4,64]{0,1,2:T(4,128)(2,1)S(1)} %copy.104), channel_id=1, replica_groups=mesh['seq'=32,'req'=8] {'seq'}, dimensions={2}, use_global_device_ids=true | all-gather | bytes 135168 | tf_op jit(solution)/shard_map/all_gather | solution.py:85
  151.0 3.8 fusion.134
  154.8 2.2 copy.129
  158.5 12.8 %all_gather.52 = bf16[2048,64]{0,1:T(8,128)(2,1)S(1)} all-gather(bf16[256,64]{0,1:T(8,128)(2,1)S(1)} %copy-done.4), channel_id=1, replica_groups=mesh['seq'=32,'req'=8] {'req'}, dimensions={0}, use_global_device_ids=true | all-gather | bytes 294912 | tf_op jit(solution)/shard_map/all_gather | solution.py:68
  171.7 50.1 %all_gather.53 = bf16[8,4,2048]{0,1,2:T(4,128)(2,1)S(1)} all-gather(bf16[8,4,64]{0,1,2:T(4,128)(2,1)S(1)} %copy.109), channel_id=1, replica_groups=mesh['seq'=32,'req'=8] {'seq'}, dimensions={2}, use_global_device_ids=true | all-gather | bytes 135168 | tf_op jit(solution)/shard_map/all_gather | solution.py:84
  223.0 2.9 select_select_fusion
  226.0 1.3 fusion.135
  231.1 47.4 %all-gather.1 = bf16[256,4,16]{2,1,0:T(4,128)(2,1)S(1)} all-gather(bf16[8,4,16]{2,1,0:T(4,128)(2,1)S(1)} %copy.116), channel_id=3, replica_groups=mesh['seq'=32,'req'=8] {'seq'}, dimensions={0}, use_global_device_ids=true | all-gather | bytes 33792 | tf_op jit(solution)/shard_map/all_gather | solution.py:12
  278.6 47.5 %all-gather = bf16[256,4,16]{2,1,0:T(4,128)(2,1)S(1)} all-gather(bf16[8,4,16]{2,1,0:T(4,128)(2,1)S(1)} %copy.114), channel_id=2, replica_groups=mesh['seq'=32,'req'=8] {'seq'}, dimensions={0}, use_global_device_ids=true | all-gather | bytes 33792 | tf_op jit(solution)/shard_map/all_gather | solution.py:12
  326.1 12.8 %all_gather.60 = bf16[2048,64]{0,1:T(8,128)(2,1)S(1)} all-gather(bf16[256,64]{0,1:T(8,128)(2,1)S(1)} %copy-done.5), channel_id=1, replica_groups=mesh['seq'=32,'req'=8] {'req'}, dimensions={0}, use_global_device_ids=true | all-gather | bytes 294912 | tf_op jit(solution)/shard_map/all_gather | solution.py:71
  339.9 38.4 %while.19 = (s32[]{:T(128)}, f32[8,4,16]{2,1,0:T(4,128)S(1)}, f32[8,4,16]{2,1,0:T(4,128)S(1)}, f32[8,4,16,128]{3,2,1,0:T(8,128)S(1)}, bf16[32,8,4,16]{3,2,1,0:T(...) while((s32[]{:T(128)}, f32[8,4,16]{2,1,0:T(4,128)S(1)}, ...), condition=%wide.region_5.6_spmd, body=%wide.region_4.5_spmd.sunk | while | flops 266245 | bytes 673943 | solution.py:20
  339.9 1.2 fusion.143
  341.2 1.2 fusion.143
  342.4 1.2 fusion.143
  343.7 1.2 fusion.143
  344.9 1.2 fusion.143
  346.1 1.2 fusion.143
  347.4 1.2 fusion.143
  348.6 1.2 fusion.143
  349.8 1.2 fusion.143
  351.1 1.2 fusion.143
  352.3 1.2 fusion.143
  353.6 1.2 fusion.143
  354.8 1.2 fusion.143
  356.1 1.2 fusion.143
  357.3 1.2 fusion.143
  358.5 1.2 fusion.143
  359.8 1.2 fusion.143
  361.0 1.2 fusion.143
  362.2 1.2 fusion.143
  363.5 1.2 fusion.143
  364.7 1.2 fusion.143
  365.9 1.2 fusion.143
  367.2 1.2 fusion.143
  368.4 1.2 fusion.143
  372.1 1.2 fusion.143
  377.1 1.2 fusion.143
  378.9 50.4 %all_gather.61 = bf16[8,4,2048]{0,1,2:T(4,128)(2,1)S(1)} all-gather(bf16[8,4,64]{0,1,2:T(4,128)(2,1)S(1)} %copy.124), channel_id=1, replica_groups=mesh['seq'=32,'req'=8] {'seq'}, dimensions={2}, use_global_device_ids=true | all-gather | bytes 135168 | tf_op jit(solution)/shard_map/all_gather | solution.py:120
  430.9 1.6 fusion.94
  432.5 2.2 convolution_convert_fusion
  434.7 78.5 %all-gather.15.cloned.1.call-done = bf16[256,4,2048]{2,0,1:T(8,128)(2,1)} async-done(((bf16[8,4,2048]{2,0,1:T(8,128)(2,1)}), bf16[256,4,2048]{2,0,1:T(8,128)(2,1)}) %all-gather.15.cloned.1.call-update) | async-done | bytes 4194320 | tf_op jit(solution)/shard_map/all_gather | solution.py:131
  513.3 2.9 bitcast_reduce_fusion
  (121 shorter events, 23.5 us)
Async XLA Ops:
  7.2 331.8 %all-gather.13.cloned.1.call-start = ((), (), s32[]{:S(2)}) async-start(), calls=%async_computation.2 | async-start | bytes 4325376 | tf_op jit(solution)/shard_map/all_gather | solution.py:12
  83.9 3.7 copy-start.3
  83.9 16.6 %copy-start = (bf16[8,4,2048]{2,1,0:T(4,128)(2,1)S(1)}, bf16[8,4,2048]{2,1,0:T(4,128)(2,1)}, u32[]{:S(2)}) copy-start(bf16[8,4,2048]{2,1,0:T(4,128)(2,1)} %param.22) | copy-start | bytes 393220
  83.9 16.6 %copy-start.11 = (f32[2048]{0:T(1024)S(1)}, f32[2048]{0:T(1024)}, u32[]{:S(2)}) copy-start(f32[2048]{0:T(1024)} %param.27) | copy-start | bytes 24580
  83.9 16.6 %copy-start.12 = (f32[2048]{0:T(1024)S(1)}, f32[2048]{0:T(1024)}, u32[]{:S(2)}) copy-start(f32[2048]{0:T(1024)} %param.26) | copy-start | bytes 24580
  83.9 16.6 %copy-start.13 = (f32[64]{0:T(128)S(1)}, f32[64]{0:T(128)}, u32[]{:S(2)}) copy-start(f32[64]{0:T(128)} %param.31) | copy-start | bytes 772
  154.8 3.7 copy-start.4
  154.8 16.5 %copy-start.14 = (f32[64]{0:T(128)S(1)}, f32[64]{0:T(128)}, u32[]{:S(2)}) copy-start(f32[64]{0:T(128)} %param.29) | copy-start | bytes 772
  171.7 51.2 %copy-start.9 = (s32[8]{0:T(128)S(1)}, s32[8]{0:T(128)}, u32[]{:S(2)}) copy-start(s32[8]{0:T(128)} %param.23) | copy-start | bytes 100
  226.0 2.0 copy-start.1
  226.0 2.0 copy-start.2
  227.2 98.8 %copy-start.5 = (bf16[256,64]{0,1:T(8,128)(2,1)S(1)}, bf16[256,64]{0,1:T(8,128)(2,1)}, u32[]{:S(2)}) copy-start(bf16[256,64]{0,1:T(8,128)(2,1)} %param.34) | copy-start | bytes 98308
  228.7 202.1 %all-gather.9.cloned.1.call-start = ((), (), s32[]{:S(2)}) async-start(), calls=%async_computation | async-start | bytes 1179648 | tf_op jit(solution)/shard_map/all_gather | solution.py:72
  229.5 203.0 %all-gather.11.cloned.1.call-start = ((), (), s32[]{:S(2)}) async-start(), calls=%async_computation.1 | async-start | bytes 1179648 | tf_op jit(solution)/shard_map/all_gather | solution.py:128
  230.2 283.1 %all-gather.15.cloned.1.call-start = ((), (), s32[]{:S(2)}) async-start(), calls=%async_computation.3 | async-start | bytes 4325376 | tf_op jit(solution)/shard_map/all_gather | solution.py:131
  339.9 38.6 %copy-start.15 = (f32[64]{0:T(128)S(1)}, f32[64]{0:T(128)}, u32[]{:S(2)}) copy-start(f32[64]{0:T(128)} %param.35) | copy-start | bytes 772
  378.8 52.1 %copy-start.6 = (f32[2048]{0:T(1024)S(1)}, f32[2048]{0:T(1024)}, u32[]{:S(2)}) copy-start(f32[2048]{0:T(1024)} %param.37) | copy-start | bytes 24580
  378.8 52.1 %copy-start.7 = (f32[2048]{0:T(1024)S(1)}, f32[2048]{0:T(1024)}, u32[]{:S(2)}) copy-start(f32[2048]{0:T(1024)} %param.36) | copy-start | bytes 24580
  378.8 52.0 %copy-start.10 = (f32[256]{0:T(256)S(1)}, f32[256]{0:T(256)}, u32[]{:S(2)}) copy-start(f32[256]{0:T(256)} %param.39) | copy-start | bytes 3076
  434.7 81.4 %copy-start.8 = (f32[2048]{0:T(1024)S(1)}, f32[2048]{0:T(1024)}, u32[]{:S(2)}) copy-start(f32[2048]{0:T(1024)} %param.41) | copy-start | bytes 24580
Sparse Core Ops, SparseCore 0:
  228.8 78.4 all-gather.12
  309.2 24.8 all-gather.8
  335.9 25.9 all-gather.10
  434.9 78.3 all-gather.14
